TPU v7x, 256 devices: a whole 4x4x8 slice. The times are simulated.
256 devices in a mesh: band: 4 (over x), ga: 64 (over z, y, core).
Axes of the slice: x: 4, y: 4, z: 8, core: 2. Of those that a mesh axis runs over, the one named last changes fastest.
Arguments:
- psi_valence: bfloat16 [2, 2, 128, 18432], P(None, None, 'ga'), may hold values from -6 to 6
- psi_conduction: bfloat16 [2, 128, 128, 18432], P(None, 'band', 'ga'), may hold values from -6 to 6
- val_energy: float32 [2], replicated, may hold values from -2 to -0.5
- cond_energy: float32 [128], P('band'), may hold values from 0.3 to 10
- miller: int32 [3, 40960], P(None, 'ga'), may hold values from -96 to 95, as said below
- pair_list: int32 [2, 32], P(None, 'band'), may hold values from 0 to 127, as said below
Outputs:
- chi_slab: float32 [1024, 2, 40960], P('band', None, 'ga')
Inputs may be any that keep to these rules, and one draw needn't show every extreme that they name: `miller`: rows 0, 1, 2 hold h in [-64, 64), k in [-48, 48), l in [-96, 96). The G vectors of columns j * 640 to (j + 1) * 640 - 1 are distinct and have (k mod 96) * 192 + (l mod 192) in [j * 288, (j + 1) * 288). `pair_list`: columns b * 8 to (b + 1) * 8 - 1 name distinct pairs, with row 0 a valence band below 2 and row 1 a conduction band in [b * 32, (b + 1) * 32); each such block holds the pair of the highest valence band, number 1, with conduction band (b + 1) * 32 - 1.
All inputs are finite; a program needn't handle non-finite values.
Results may differ from a plain program's by a relative error of at most 0.0003.
Values sent between devices are 32-bit elements; how exact they have to be, the bound alone decides.
A program may use at most 128 MiB of HBM per device.

v0:
```python
import math

import jax
import jax.numpy as jnp
from jax import lax
from jax.sharding import PartitionSpec as P

NX = 128
NY = 96
NZ = 192
ROW_DEV = 16


HIGHEST = lax.Precision.HIGHEST


def dft_tables(length):
    points = jnp.arange(length, dtype=jnp.int32)
    product = points[:, None] * points[None, :] % length
    angles = product.astype(jnp.float32) * (2.0 * math.pi / length)
    return (jnp.cos(angles), jnp.sin(angles))


def transform(real_part, imag_part, formula, length):
    cosine_table, sine_table = dft_tables(length)
    real_new = jnp.einsum(formula, real_part, cosine_table, precision=HIGHEST) + jnp.einsum(
        formula, imag_part, sine_table, precision=HIGHEST
    )
    imag_new = jnp.einsum(formula, imag_part, cosine_table, precision=HIGHEST) - jnp.einsum(
        formula, real_part, sine_table, precision=HIGHEST
    )
    return (real_new, imag_new)


def pick_valence(psi_valence, choose):
    picked = jnp.zeros((2, choose.shape[0]) + psi_valence.shape[2:], jnp.float32)
    for number in range(psi_valence.shape[1]):
        picked = jnp.where(
            (choose == number)[None, :, None, None],
            psi_valence[:, number][:, None].astype(jnp.float32),
            picked,
        )
    return picked


def pick_energy(val_energy, choose):
    picked = jnp.zeros(choose.shape, jnp.float32)
    for number in range(val_energy.shape[0]):
        picked = jnp.where(choose == number, val_energy[number], picked)
    return picked


def gram_block(left_real, left_imag, right_real, right_imag):
    part_real = jnp.einsum("qr,qg->rg", left_real, right_real, precision=HIGHEST) + jnp.einsum(
        "qr,qg->rg", left_imag, right_imag, precision=HIGHEST
    )
    part_imag = jnp.einsum("qr,qg->rg", left_imag, right_real, precision=HIGHEST) - jnp.einsum(
        "qr,qg->rg", left_real, right_imag, precision=HIGHEST
    )
    return jnp.stack([part_real, part_imag], axis=1)


def per_device(psi_valence, psi_conduction, val_energy, cond_energy, miller, pair_list):
    band_index = lax.axis_index("band")
    band_count = lax.axis_size("band")
    ga_index = lax.axis_index("ga")
    ga_count = lax.axis_size("ga")
    cond_local = psi_conduction.shape[1]
    pair_count = pair_list.shape[1]
    plane_count = psi_conduction.shape[2]
    valence_choice = pair_list[0]
    cond_choice = pair_list[1] - band_index * cond_local
    valence = pick_valence(psi_valence, valence_choice)
    conduction = jnp.take(psi_conduction, cond_choice, axis=1).astype(jnp.float32)
    dens_real = valence[0] * conduction[0] + valence[1] * conduction[1]
    dens_imag = valence[0] * conduction[1] - valence[1] * conduction[0]
    grid_shape = (pair_count, plane_count, NY, NZ)
    dens_real, dens_imag = transform(
        dens_real.reshape(grid_shape), dens_imag.reshape(grid_shape), "pxyz,kz->pxyk", NZ
    )
    dens_real, dens_imag = transform(dens_real, dens_imag, "pxyz,ky->pxkz", NY)
    flat_shape = (pair_count, plane_count, NY * NZ)
    dens_real = dens_real.reshape(flat_shape)
    dens_imag = dens_imag.reshape(flat_shape)
    pencil_count = NY * NZ // ga_count
    norm_factor = 1.0 / math.sqrt(NX * NY * NZ)
    line_local = jnp.mod(miller[1], NY) * NZ + jnp.mod(miller[2], NZ) - ga_index * pencil_count
    positions = jnp.mod(miller[0], NX) * pencil_count + line_local
    real_part, imag_part = transform(
        lax.all_to_all(dens_real, "ga", split_axis=2, concat_axis=1, tiled=True),
        lax.all_to_all(dens_imag, "ga", split_axis=2, concat_axis=1, tiled=True),
        "pxq,kx->pkq",
        NX,
    )
    item_count = real_part.shape[0]
    real_flat = real_part.reshape(item_count, -1)
    imag_flat = imag_part.reshape(item_count, -1)
    amp_real = jnp.take(real_flat, positions, axis=1) * norm_factor
    amp_imag = jnp.take(imag_flat, positions, axis=1) * norm_factor
    weights = 4.0 / (
        (pick_energy(val_energy, valence_choice) - jnp.take(cond_energy, cond_choice))
        * math.sqrt(pair_count * band_count)
    )
    rows_real = amp_real[:, :ROW_DEV] * weights[:, None]
    rows_imag = amp_imag[:, :ROW_DEV] * weights[:, None]
    rows_real, rows_imag = (
        lax.all_gather(rows_real, "ga", axis=1, tiled=True),
        lax.all_gather(rows_imag, "ga", axis=1, tiled=True),
    )
    return lax.psum_scatter(
        gram_block(rows_real, rows_imag, amp_real, amp_imag),
        "band",
        scatter_dimension=0,
        tiled=True,
    )


def solution(mesh):
    return jax.shard_map(
        per_device,
        mesh=mesh,
        in_specs=(
            P(None, None, "ga", None),
            P(None, "band", "ga", None),
            P(),
            P("band"),
            P(None, "ga"),
            P(None, "band"),
        ),
        out_specs=P("band", None, "ga"),
        check_vma=False,
    )
```

profile of v0, /device:TPU:1, one launch (start us, length us, event | category | flops | bytes accessed | tf_op | source)
XLA Modules:
  0.0 486.2 jit_solution(15604545694588437283)
XLA Ops:
  6.5 0.7 compare_bitcast_fusion
  7.2 0.7 fusion.86
  7.9 1.3 fusion.127
  9.2 1.2 bitcast_convert_fusion.1
  10.4 0.0 copy-start.6
  10.5 0.6 gather_fusion.1
  11.1 5.3 %gather_fusion = bf16[8,2,2,18432]{3,2,1,0:T(2,128)(2,1)S(1)} fusion(bf16[2,32,2,18432]{3,2,1,0:T(2,128)(2,1)} %param.9, s32[1024]{0:T(1024)S(1)} %pad_clamp_fusion.1), kind=kCustom, calls=%fused_computation.2 | custom fusion | bytes 2359328 | tf_op jit(solution)/shard_map/jit(_take)/gather | solution.py:74
  16.4 1.2 multiply_divide_fusion
  17.6 1.1 convert_bitcast_fusion
  18.7 1.1 select_select_fusion
  19.9 2.1 multiply_add_fusion
  21.9 1.1 add.114
  23.1 2.4 sub.67
  25.5 2.1 fusion.6
  27.7 2.1 fusion.8
  29.8 2.2 convolution_subtract_fusion
  32.1 2.2 convolution_add_fusion
  34.3 1.6 fusion.49
  36.0 3.4 add_bitcast_fusion.1
  39.3 18.3 %copy.65 = f32[8,2,96,192]{0,1,3,2:T(2,128)} copy(f32[8,2,96,192]{3,2,1,0:T(8,128)} %add_bitcast_fusion.1) | data formatting | bytes 2359296 | tf_op jit(solution)/shard_map/reshape | solution.py:83
  57.6 28.4 %reshape.162 = f32[64,1,4608]{2,1,0:T(1,128)} reshape(f32[18432,2,8]{2,1,0:T(2,128)} %bitcast.131) | data formatting | bytes 2359296
  85.9 13.3 %all-to-all-start = ((f32[64,1,4608]{2,1,0:T(1,128)}), f32[64,1,4608]{2,1,0:T(1,128)}, u32[]{:S(2)}, u32[]{:S(2)}) async-start(f32[64,1,4608]{2,1,0:T(1,128)} %reshape.162), calls=%async_computation | async-start | bytes 2359296 | tf_op jit(solution)/shard_map/all_to_all | solution.py:90
  99.3 1.6 fusion.47
  100.9 1.7 subtract_bitcast_fusion.1
  102.6 16.3 %copy.68 = f32[8,2,96,192]{0,1,3,2:T(2,128)} copy(f32[8,2,96,192]{3,2,1,0:T(8,128)S(1)} %subtract_bitcast_fusion.1) | data formatting | bytes 2359296 | tf_op jit(solution)/shard_map/reshape | solution.py:84
  118.9 28.3 %reshape.160 = f32[64,1,4608]{2,1,0:T(1,128)} reshape(f32[18432,2,8]{2,1,0:T(2,128)} %bitcast.132) | data formatting | bytes 2359296
  147.3 10.6 %all-to-all-start.1 = ((f32[64,1,4608]{2,1,0:T(1,128)}), f32[64,1,4608]{2,1,0:T(1,128)}, u32[]{:S(2)}, u32[]{:S(2)}) async-start(f32[64,1,4608]{2,1,0:T(1,128)} %reshape.160), calls=%async_computation.1 | async-start | bytes 2359296 | tf_op jit(solution)/shard_map/all_to_all | solution.py:91
  157.9 0.0 reduce-scatter.2.cloned.1.call-start
  158.0 0.5 broadcast.243
  158.6 4.7 reduce.6
  163.3 30.2 %reshape.163 = f32[18432,2,8]{2,1,0:T(2,128)} reshape(f32[64,4608]{1,0:T(8,128)S(1)} %reduce.6) | data formatting | bytes 2359296
  193.5 21.7 %copy.67 = f32[8,2,64,288]{3,0,1,2:T(8,128)S(1)} copy(f32[8,2,64,288]{0,1,3,2:T(2,128)} %bitcast.133) | data formatting | bytes 2359296 | tf_op jit(solution)/shard_map/all_to_all | solution.py:90
  215.2 0.5 copy.45
  215.7 2.3 fusion.38
  218.1 4.7 reduce.7
  222.8 30.0 %reshape.161 = f32[18432,2,8]{2,1,0:T(2,128)} reshape(f32[64,4608]{1,0:T(8,128)S(1)} %reduce.7) | data formatting | bytes 2359296
  252.8 23.2 %copy.70 = f32[8,2,64,288]{3,0,1,2:T(8,128)} copy(f32[8,2,64,288]{0,1,3,2:T(2,128)} %bitcast.134) | data formatting | bytes 2359296 | tf_op jit(solution)/shard_map/all_to_all | solution.py:91
  276.0 1.9 copy.49
  277.9 0.0 copy-start.4
  277.9 1.3 fusion.36
  279.2 1.4 fusion.1
  280.6 1.4 fusion
  282.0 9.5 %copy.72 = f32[8,128,288]{0,2,1:T(8,128)} copy(f32[8,128,288]{1,2,0:T(8,128)S(1)} %fusion) | data formatting | bytes 2359296 | tf_op jit(solution)/shard_map/reshape | solution.py:97
  291.4 9.6 %copy.71 = f32[8,128,288]{0,2,1:T(8,128)} copy(f32[8,128,288]{1,2,0:T(8,128)S(1)} %fusion.1) | data formatting | bytes 2359296 | tf_op jit(solution)/shard_map/reshape | solution.py:96
  301.0 8.0 %gather_fusion.3 = f32[640,8]{1,0:T(8,128)S(1)} fusion(f32[8,36864]{0,1:T(8,128)} %bitcast.136, s32[1024]{0:T(1024)S(1)} %pad_clamp_fusion), kind=kCustom, calls=%fused_computation.1.clone | custom fusion | bytes 43520 | tf_op jit(solution)/shard_map/jit(_take)/gather | solution.py:99
  309.1 8.0 %gather_fusion.2 = f32[640,8]{1,0:T(8,128)S(1)} fusion(f32[8,36864]{0,1:T(8,128)} %bitcast.135, s32[1024]{0:T(1024)S(1)} %pad_clamp_fusion), kind=kCustom, calls=%fused_computation.clone | custom fusion | bytes 43520 | tf_op jit(solution)/shard_map/jit(_take)/gather | solution.py:98
  317.1 0.2 bitcast_multiply_fusion.1
  317.3 0.1 copy.52
  317.3 0.1 copy.58
  317.4 45.1 %all-gather.1 = f32[64,16,8]{1,2,0:T(8,128)S(1)} all-gather(f32[1,16,8]{1,2,0:T(8,128)S(1)} %bitcast.140), channel_id=1, replica_groups=mesh['band'=4,'ga'=64] {'ga'}, dimensions={0}, use_global_device_ids=true | all-gather | bytes 33280 | tf_op jit(solution)/shard_map/all_gather | solution.py:108
  362.5 0.1 copy.59
  362.5 0.2 reshape.146
  362.7 43.0 %all-gather = f32[64,16,8]{1,2,0:T(8,128)S(1)} all-gather(f32[1,16,8]{1,2,0:T(8,128)S(1)} %bitcast.139), channel_id=1, replica_groups=mesh['band'=4,'ga'=64] {'ga'}, dimensions={0}, use_global_device_ids=true | all-gather | bytes 33280 | tf_op jit(solution)/shard_map/all_gather | solution.py:107
  405.7 0.1 copy.53
  405.8 0.2 reshape.144
  405.9 2.7 fusion.128
  408.6 2.7 fusion.129
  411.3 2.8 add_bitcast_fusion
  414.1 2.8 subtract_bitcast_fusion
  417.0 2.6 pad_maximum_fusion
  419.6 0.0 reduce-scatter.2.cloned.1.call-update
  419.6 0.0 copy-start.1
  419.6 55.9 %reduce-scatter.2.cloned.1.call-done = f32[256,2,640]{2,0,1:T(8,128)} async-done(((f32[1024,2,640]{2,0,1:T(8,128)}), f32[256,2,640]{2,0,1:T(8,128)}) %reduce-scatter.2.cloned.1.call-update) | async-done | bytes 1310736 | tf_op jit(solution)/shard_map/reduce_scatter | solution.py:110
  475.6 3.4 copy.60
  (18 shorter events, 0.1 us)
Async XLA Ops:
  6.5 3.9 copy-start
  10.4 5.9 %copy-start.6 = (s32[2,8]{1,0:T(2,128)S(1)}, s32[2,8]{1,0:T(2,128)}, u32[]{:S(2)}) copy-start(s32[2,8]{1,0:T(2,128)} %param.13) | copy-start | bytes 196
  25.5 2.2 copy-start.2
  29.8 2.2 copy-start.3
  85.9 61.3 %all-to-all-start = ((f32[64,1,4608]{2,1,0:T(1,128)}), f32[64,1,4608]{2,1,0:T(1,128)}, u32[]{:S(2)}, u32[]{:S(2)}) async-start(f32[64,1,4608]{2,1,0:T(1,128)} %reshape.162), calls=%async_computation | async-start | bytes 2359296 | tf_op jit(solution)/shard_map/all_to_all | solution.py:90
  147.3 10.7 %copy-start.5 = (s32[3,640]{1,0:T(4,128)S(1)}, s32[3,640]{1,0:T(4,128)}, u32[]{:S(2)}) copy-start(s32[3,640]{1,0:T(4,128)} %param.12) | copy-start | bytes 23044
  147.3 70.8 %all-to-all-start.1 = ((f32[64,1,4608]{2,1,0:T(1,128)}), f32[64,1,4608]{2,1,0:T(1,128)}, u32[]{:S(2)}, u32[]{:S(2)}) async-start(f32[64,1,4608]{2,1,0:T(1,128)} %reshape.160), calls=%async_computation.1 | async-start | bytes 2359296 | tf_op jit(solution)/shard_map/all_to_all | solution.py:91
  157.9 317.7 %reduce-scatter.2.cloned.1.call-start = ((), (), s32[]{:S(2)}) async-start(), calls=%async_computation.3 | async-start | bytes 6553600 | tf_op jit(solution)/shard_map/reduce_scatter | solution.py:110
  277.9 1.4 copy-start.4
  419.6 59.3 %copy-start.1 = (f32[32]{0:T(128)S(1)}, f32[32]{0:T(128)}, u32[]{:S(2)}) copy-start(f32[32]{0:T(128)} %param.11) | copy-start | bytes 388
Sparse Core Ops, SparseCore 0:
  419.7 55.7 reduce-scatter.1
where the time goes:
time: 495 us; the launch traced here: 486 us
  local copies, waits for them, and re-layouts  249 us (50%)
  blocking collectives  88.1 us (18%)
  waiting for transfers between devices  56 us (11%)
  matrix products  34.5 us (7%)
  starting transfers between devices  24 us (5%)
  other arithmetic  20.4 us (4%)
  between operations  14.2 us (3%)
    unnamed x22, local copies, waits for them, and re-layouts  117 us
    reduce_scatter x1, waiting for transfers between devices, per_device(): lax.psum_scatter(gram_block(rows_real, rows_imag, amp_real, amp_imag), 'b...  55.9 us
    all_gather x1, blocking collectives, per_device(): lax.all_gather(rows_imag, 'ga', axis=1, tiled=True)  45.1 us
    all_gather x1, blocking collectives, per_device(): lax.all_gather(rows_real, 'ga', axis=1, tiled=True)  43 us
    all_to_all x2, local copies, waits for them, and re-layouts, per_device(): lax.all_to_all(dens_imag, 'ga', split_axis=2, concat_axis=1, tiled=True)  25 us
    all_to_all x3, local copies, waits for them, and re-layouts, per_device(): lax.all_to_all(dens_real, 'ga', split_axis=2, concat_axis=1, tiled=True)  22.8 us
    reshape x1, local copies, waits for them, and re-layouts, per_device(): dens_real = dens_real.reshape(flat_shape)  18.3 us
    reshape x1, local copies, waits for them, and re-layouts, per_device(): dens_imag = dens_imag.reshape(flat_shape)  16.3 us
  transfers between devices with their start and end apart: 3, of which 1 were waited for; matrix products, arithmetic and copies ran while one was open for 22% of the time, Pallas kernels for 0%

commit v1 on v0

v1 whole, which is shorter than its diff:
```python
import math

import jax
import jax.numpy as jnp
import numpy as np
from jax import lax
from jax.experimental import pallas as pl
from jax.experimental.pallas import tpu as pltpu
from jax.sharding import PartitionSpec as P

NX = 128
NY = 96
NZ = 192
ROW_DEV = 16
PAIRS = 8
GA = 64
ZN, YN, CN, BN = 8, 4, 2, 4
HALF_Y = NY // 2
PENCILS = NY * NZ // GA
G_DEV = 640
TILES = G_DEV // 128
MESH = pl.DeviceIdType.MESH
F32 = jnp.float32
BF16 = jnp.bfloat16


def split_np(table):
    high = table.astype(np.float32).astype(jnp.bfloat16)
    low = (table - high.astype(np.float64)).astype(jnp.bfloat16)
    return high, low


def z_table():
    points = np.arange(NZ)
    angle = 2.0 * np.pi * ((points[:, None] * points[None, :]) % NZ) / NZ
    cosine, sine = np.cos(angle), np.sin(angle)
    table = np.zeros((2, 512, 512))
    for parity in range(2):
        first = 64 * parity
        table[parity, first : first + NZ, 0:NZ] = cosine
        table[parity, first : first + NZ, 256 : 256 + NZ] = -sine
        table[parity, 256 + first : 256 + first + NZ, 0:NZ] = sine
        table[parity, 256 + first : 256 + first + NZ, 256 : 256 + NZ] = cosine
    return table


def y_table():
    k = np.arange(NY)[:, None]
    table = np.zeros((2, NY, 2, 2, HALF_Y))
    for parity in range(2):
        y = 2 * np.arange(HALF_Y)[None, :] + parity
        angle = 2.0 * np.pi * ((k * y) % NY) / NY
        table[0, :, 0, parity] = np.cos(angle)
        table[0, :, 1, parity] = np.sin(angle)
        table[1, :, 0, parity] = -np.sin(angle)
        table[1, :, 1, parity] = np.cos(angle)
    return table.reshape(2 * NY, 4 * HALF_Y)


def x_table():
    angle = 2.0 * np.pi * np.arange(NX) / NX
    norm = 1.0 / math.sqrt(NX * NY * NZ)
    table = np.stack([np.cos(angle), np.sin(angle)]) * norm
    return np.repeat(table[:, None, :], 8, axis=1).astype(np.float32)


def split(value):
    high = value.astype(BF16)
    low = (value - high.astype(F32)).astype(BF16)
    return high, low


def dot(a, b):
    return jnp.dot(a, b, preferred_element_type=F32)


def dot3(a_high, a_low, b_high, b_low):
    return dot(a_high, b_high) + (dot(a_high, b_low) + dot(a_low, b_high))


def coordinates():
    band = lax.axis_index("band")
    ga = lax.axis_index("ga")
    return band, ga // 8, (ga // 2) % 4, ga % 2


def device(band, z, y, c):
    return (band, z * 8 + y * 2 + c)


def greet(partners):
    barrier = pltpu.get_barrier_semaphore()
    for partner in partners:
        pl.semaphore_signal(barrier, inc=1, device_id=partner, device_id_type=MESH)
    pl.semaphore_wait(barrier, len(partners))


def send(src, dst, send_sem, recv_sem, partner):
    copy = pltpu.make_async_remote_copy(
        src_ref=src, dst_ref=dst, send_sem=send_sem, recv_sem=recv_sem, device_id=partner, device_id_type=MESH
    )
    copy.start()
    return copy


def miller_kernel(mine_ref, out_ref, all_ref, send_sem, recv_sem):
    band, z, y, c = coordinates()
    z_partners = [device(band, (z + d) % ZN, y, c) for d in range(1, ZN)]
    y_partners = [device(band, z, (y + d) % YN, c) for d in range(1, YN)]
    core_partner = device(band, z, y, 1 - c)
    greet(z_partners + y_partners + [core_partner])
    all_ref[z, y, c] = mine_ref[...]
    copies = []
    for n, partner in enumerate(z_partners):
        block = all_ref.at[z, y, c]
        copies.append(send(block, block, send_sem.at[n], recv_sem.at[n], partner))
    for copy in copies:
        copy.wait()
    copies = []
    for n, partner in enumerate(y_partners):
        block = all_ref.at[:, y, c]
        copies.append(send(block, block, send_sem.at[7 + n], recv_sem.at[7 + n], partner))
    for copy in copies:
        copy.wait()
    block = all_ref.at[:, :, c]
    send(block, block, send_sem.at[10], recv_sem.at[10], core_partner).wait()
    out_ref[...] = all_ref[...]


def gather_miller(mine):
    shape = (ZN, YN, CN, 2, G_DEV)
    vmem = pl.BlockSpec(memory_space=pltpu.VMEM)
    return pl.pallas_call(
        miller_kernel,
        out_shape=jax.ShapeDtypeStruct(shape, jnp.int32),
        in_specs=[vmem],
        out_specs=vmem,
        scratch_shapes=[
            pltpu.VMEM(shape, jnp.int32),
            pltpu.SemaphoreType.DMA((11,)),
            pltpu.SemaphoreType.DMA((11,)),
        ],
        compiler_params=pltpu.CompilerParams(collective_id=0, has_side_effects=True),
        name="miller_gather",
    )(mine)


def density_step(y2, pair_ref, cond_start, pv_ref, pc_ref, dens):
    lanes = pl.ds(pl.multiple_of(y2 * 384, 384), 384)
    for p in range(PAIRS):
        v = pair_ref[0, p]
        q = pair_ref[1, p] - cond_start
        vr = pv_ref[0, v, :, lanes].astype(F32)
        vi = pv_ref[1, v, :, lanes].astype(F32)
        cr = pc_ref[0, q, :, lanes].astype(F32)
        ci = pc_ref[1, q, :, lanes].astype(F32)
        rows = slice(2 * p, 2 * p + 2)
        dens[y2, rows, 0:384] = vr * cr + vi * ci
        dens[y2, rows, 384:768] = vr * ci - vi * cr


def partial_kernel(
    pair_ref, val_ref, cond_ref, pv_ref, pc_ref, wzh_ref, wzl_ref, wyh_ref, wyl_ref, wx_ref, miller_ref, out_ref, dens, zed, spec
):
    band = lax.axis_index("band")
    ga = lax.axis_index("ga")
    cond_start = band * 32

    @pl.loop(0, HALF_Y)
    def _(y2):
        density_step(y2, pair_ref, cond_start, pv_ref, pc_ref, dens)

    @pl.loop(0, 6)
    def _(block):
        rows = pl.ds(pl.multiple_of(block * 128, 128), 128)
        for parity in range(2):
            first = 128 * parity
            span = pl.ds(block * 8, 8)
            both = jnp.concatenate([dens[span, :, first : first + 256], dens[span, :, 384 + first : 640 + first]], axis=2)
            high, low = split(both.reshape(128, 512))
            result = dot3(high, low, wzh_ref[parity], wzl_ref[parity])
            for tile in range(4):
                zed[parity, tile, rows, :] = result[:, 128 * tile : 128 * tile + 128]

    for p in range(PAIRS):
        for plane in range(2):
            row = 2 * p + plane
            halves = [
                jnp.concatenate(
                    [
                        zed[parity, 2 * part + tile, pl.ds(row, HALF_Y, stride=16), :]
                        for part in range(2)
                        for parity in range(2)
                    ],
                    axis=0,
                )
                for tile in range(2)
            ]
            high, low = split(jnp.concatenate(halves, axis=1))
            result = dot3(wyh_ref[...], wyl_ref[...], high, low)
            for part in range(2):
                for tile in range(2):
                    spec[tile, pl.ds(part * 16 + plane * 8 + p, NY, stride=32), :] = result[
                        part * NY : (part + 1) * NY, 128 * tile : 128 * tile + 128
                    ]

    pair_rows = lax.broadcasted_iota(jnp.int32, (8, 128), 0)
    gap = jnp.ones((8, 128), F32)
    for p in range(PAIRS):
        value = cond_ref[pair_ref[1, p] - cond_start] - val_ref[pair_ref[0, p]]
        gap = jnp.where(pair_rows == p, value, gap)
    scale = jnp.sqrt(4.0 / (gap * math.sqrt(32.0)))
    x0 = 2 * ga
    cos_tab = wx_ref[0]
    sin_tab = wx_ref[1]

    def take(table, index):
        return jnp.take_along_axis(table, index, axis=1)

    @pl.loop(0, ZN * YN)
    def _(m):
        zd = m // YN
        yd = m % YN
        base = pl.multiple_of(m * 96, 96)
        for cd in range(2):
            tiles = ((0, 0), (0, 1), (1, 0)) if cd == 0 else ((1, 0), (1, 1), (2, 0), (2, 1))
            for g in range(TILES):
                lanes = slice(128 * g, 128 * g + 128)
                line = jnp.broadcast_to(miller_ref[zd, yd, cd, 0:1, lanes], (8, 128)) + 288 * cd
                h = jnp.broadcast_to(miller_ref[zd, yd, cd, 1:2, lanes], (8, 128))
                k_low = 0 if cd == 0 else 1
                k_step = (line >= (k_low + 1) * NZ).astype(jnp.int32)
                l = line - k_low * NZ - k_step * NZ
                index = l & 127
                code = 2 * k_step + (l >> 7)
                got = []
                for group in range(4):
                    value = None
                    for k_row, tile in tiles:
                        source = spec[tile, pl.ds(pl.multiple_of(base + (32 * k_row + 8 * group), 8), 8), :]
                        taken = take(source, index)
                        if value is None:
                            value = taken
                        else:
                            value = jnp.where(code == 2 * (k_row - k_low) + tile, taken, value)
                    got.append(value)
                re0, re1, im0, im1 = got
                angle0 = (h * x0) & 127
                angle1 = (angle0 + h) & 127
                c0, s0 = take(cos_tab, angle0), take(sin_tab, angle0)
                c1, s1 = take(cos_tab, angle1), take(sin_tab, angle1)
                out_re = (c0 * re0 + s0 * im0) + (c1 * re1 + s1 * im1)
                out_im = (c0 * im0 - s0 * re0) + (c1 * im1 - s1 * re1)
                out_ref[cd, yd, zd, 0:8, lanes] = out_re * scale
                out_ref[cd, yd, zd, 8:16, lanes] = out_im * scale


def partial_sums(pair_list, val_energy, cond_energy, psi_valence, psi_conduction, miller_all):
    vmem = pl.BlockSpec(memory_space=pltpu.VMEM)
    smem = pl.BlockSpec(memory_space=pltpu.SMEM)
    wzh, wzl = split_np(z_table())
    wyh, wyl = split_np(y_table())
    tables = [jnp.asarray(t) for t in (wzh, wzl, wyh, wyl, x_table())]
    return pl.pallas_call(
        partial_kernel,
        out_shape=jax.ShapeDtypeStruct((CN, YN, ZN, 16, G_DEV), F32),
        in_specs=[smem] * 3 + [vmem] * 8,
        out_specs=vmem,
        scratch_shapes=[
            pltpu.VMEM((HALF_Y, 16, 768), F32),
            pltpu.VMEM((2, 4, 768, 128), F32),
            pltpu.VMEM((2, NY * 32, 128), F32),
        ],
        compiler_params=pltpu.CompilerParams(vmem_limit_bytes=56 * 1024 * 1024),
        name="partial_sums",
    )(pair_list, val_energy, cond_energy, psi_valence, psi_conduction, *tables, miller_all)


def sum_kernel(u_ref, amps_ref, rows_ref, from_core, relayed, near, far, total, by_z, amps, rows, send_sem, recv_sem):
    band, z, y, c = coordinates()
    z_partners = [device(band, (z + d) % ZN, y, c) for d in range(1, ZN)]
    core_partner = device(band, z, y, 1 - c)
    ahead = (y + 1 + 2 * c) % YN
    behind = (y + 3 - 2 * c) % YN
    across = (y + 2) % YN
    x_partners = [device((band + d) % BN, z, y, c) for d in range(1, BN)]
    to_ahead = device(band, z, ahead, c)
    to_behind = device(band, z, behind, c)
    to_across = device(band, z, across, c)
    y_partners = [to_ahead, to_behind, to_across]
    greet(z_partners + [core_partner] + y_partners + x_partners)

    core_copies = []
    order = [across, ahead, behind, y]
    for n, yd in enumerate(order):
        core_copies.append(send(u_ref.at[1 - c, yd], from_core.at[yd], send_sem.at[n], recv_sem.at[n], core_partner))

    core_copies[0].wait_recv()
    from_core[across] += u_ref[c, across]
    relay = send(from_core.at[across], relayed, send_sem.at[4], recv_sem.at[4], to_ahead)
    core_copies[1].wait_recv()
    from_core[behind] += u_ref[c, behind]
    back = send(from_core.at[behind], near, send_sem.at[5], recv_sem.at[5], to_behind)
    core_copies[2].wait_recv()
    from_core[ahead] += u_ref[c, ahead]
    relay.wait_recv()
    from_core[ahead] += relayed[...]
    forth = send(from_core.at[ahead], far, send_sem.at[6], recv_sem.at[6], to_ahead)
    core_copies[3].wait_recv()
    total[...] = from_core[y] + u_ref[c, y]
    back.wait_recv()
    total[...] += near[...]
    forth.wait_recv()
    total[...] += far[...]

    z_copies = []
    for n, partner in enumerate(z_partners):
        zd = (z + n + 1) % ZN
        z_copies.append(send(total.at[zd], by_z.at[n], send_sem.at[7 + n], recv_sem.at[7 + n], partner))
    result = total[z]
    for n, copy in enumerate(z_copies):
        copy.wait_recv()
        result = result + by_z[n]
    amps[band] = result
    x_copies = []
    for n, partner in enumerate(x_partners):
        x_copies.append(send(amps.at[band], amps.at[band], send_sem.at[14 + n], recv_sem.at[14 + n], partner))
    for copy in x_copies:
        copy.wait_recv()

    parts = [amps[b, :, 0:128] for b in range(BN)]
    for_real = [-part for part in parts]
    for_imag = [piece for part in parts for piece in (-part[8:16], part[0:8])]
    own = jnp.concatenate(for_real + for_imag, axis=0).T[0:ROW_DEV]
    z_home = 2 * band
    is_home = z // 2 == band

    @pl.when(is_home)
    def _():
        rows[z % 2, y, c] = own

    def row_copy(z2, n, partner):
        block = rows.at[z2, y, c]
        return pltpu.make_async_remote_copy(
            src_ref=block,
            dst_ref=block,
            send_sem=send_sem.at[17 + n],
            recv_sem=recv_sem.at[17 + z2],
            device_id=partner,
            device_id_type=MESH,
        )

    @pl.when(is_home)
    def _():
        for n, partner in enumerate(z_partners):
            row_copy(z % 2, n, partner).start()

    for z2 in range(2):

        @pl.when(z != z_home + z2)
        def _():
            row_copy(z2, 0, z_partners[0]).wait_recv()

    core_rows = rows.at[:, y, c]
    send(core_rows, core_rows, send_sem.at[24], recv_sem.at[19], core_partner).wait()
    y_copies = []
    for n, partner in enumerate(y_partners):
        block = rows.at[:, y]
        y_copies.append(send(block, block, send_sem.at[25 + n], recv_sem.at[20 + n], partner))
    amps_ref[...] = amps[...]
    for copy in y_copies:
        copy.wait()

    rows_ref[...] = rows[...]
    for copy in core_copies + [relay, back, forth] + z_copies + x_copies:
        copy.wait_send()

    @pl.when(is_home)
    def _():
        for n, partner in enumerate(z_partners):
            row_copy(z % 2, n, partner).wait_send()


def sum_up(partial):
    vmem = pl.BlockSpec(memory_space=pltpu.VMEM)
    block = (ZN, 16, G_DEV)
    return pl.pallas_call(
        sum_kernel,
        out_shape=(
            jax.ShapeDtypeStruct((BN, 16, G_DEV), F32),
            jax.ShapeDtypeStruct((2, YN, CN, ROW_DEV, 128), F32),
        ),
        in_specs=[vmem],
        out_specs=(vmem, vmem),
        scratch_shapes=[
            pltpu.VMEM((YN,) + block, F32),
            pltpu.VMEM(block, F32),
            pltpu.VMEM(block, F32),
            pltpu.VMEM(block, F32),
            pltpu.VMEM(block, F32),
            pltpu.VMEM((ZN - 1, 16, G_DEV), F32),
            pltpu.VMEM((BN, 16, G_DEV), F32),
            pltpu.VMEM((2, YN, CN, ROW_DEV, 128), F32),
            pltpu.SemaphoreType.DMA((28,)),
            pltpu.SemaphoreType.DMA((23,)),
        ],
        compiler_params=pltpu.CompilerParams(
            collective_id=1, has_side_effects=True, vmem_limit_bytes=32 * 1024 * 1024
        ),
        name="sum_up",
    )(partial)


def slab_kernel(rows_ref, amps_ref, out_ref):
    right_high, right_low = split(amps_ref[...].reshape(64, G_DEV))
    for part in range(2):
        left = rows_ref[...].reshape(256, 128)[:, 64 * part : 64 * part + 64]
        left_high, left_low = split(left)
        out_ref[:, part, :] = dot3(left_high, left_low, right_high, right_low)


def slab(rows, amps):
    vmem = pl.BlockSpec(memory_space=pltpu.VMEM)
    return pl.pallas_call(
        slab_kernel,
        out_shape=jax.ShapeDtypeStruct((256, 2, G_DEV), F32),
        in_specs=[vmem, vmem],
        out_specs=vmem,
        compiler_params=pltpu.CompilerParams(vmem_limit_bytes=32 * 1024 * 1024),
        name="slab",
    )(rows, amps)


def per_device(psi_valence, psi_conduction, val_energy, cond_energy, miller, pair_list):
    ga = lax.axis_index("ga")
    line = jnp.mod(miller[1], NY) * NZ + jnp.mod(miller[2], NZ) - ga * PENCILS
    mine = jnp.stack([line, jnp.mod(miller[0], NX)])
    miller_all = gather_miller(mine)
    partial = partial_sums(pair_list, val_energy, cond_energy, psi_valence, psi_conduction, miller_all)
    amps, rows = sum_up(partial)
    return slab(rows, amps)


def solution(mesh):
    return jax.shard_map(
        per_device,
        mesh=mesh,
        in_specs=(
            P(None, None, "ga", None),
            P(None, "band", "ga", None),
            P(),
            P("band"),
            P(None, "ga"),
            P(None, "band"),
        ),
        out_specs=P("band", None, "ga"),
        check_vma=False,
    )
```

time: 495 us -> 94.7 us (0.19); the launches traced: 486 us -> 94 us
  local copies, waits for them, and re-layouts: 249 us -> 1.74 us
  Pallas kernels: 0 us -> 90.8 us
  blocking collectives: 88.1 us -> 0 us
  waiting for transfers between devices: 56 us -> 0 us
  matrix products: 34.5 us -> 0 us
  starting transfers between devices: 24 us -> 0 us
  other arithmetic: 20.4 us -> 1.46 us
  between operations: 14.2 us -> 0.02 us
    unnamed x22 -> x2, local copies, waits for them, and re-layouts: 117 us -> 1.74 us
    pallas_call x0 -> x4, Pallas kernels: none -> 90.8 us  [the longest x1 43 us: sum_up(): pl.pallas_call(sum_kernel, out_shape=(jax.ShapeDtypeStruct((BN, 16, G_DEV...]
    all_gather x2 -> x0, blocking collectives: 88.1 us -> none  [the longest x1 45.1 us: per_device(): lax.all_gather(rows_imag, 'ga', axis=1, tiled=True)]
    reduce_scatter x1 -> x0, waiting for transfers between devices: 55.9 us -> none  [per_device(): lax.psum_scatter(gram_block(rows_real, rows_imag, amp_real, amp_imag), 'b...]
    reshape x4 -> x0, local copies, waits for them, and re-layouts: 53.6 us -> none  [the longest x1 18.3 us: per_device(): dens_real = dens_real.reshape(flat_shape)]
    all_to_all x5 -> x0, local copies, waits for them, and re-layouts: 47.8 us -> none  [the longest x2 25 us: per_device(): lax.all_to_all(dens_imag, 'ga', split_axis=2, concat_axis=1, tiled=True)]
    dot_general x16 -> x0, matrix products: 34.5 us -> none  [the longest x3 6.95 us: transform(): jnp.einsum(formula, imag_part, sine_table, precision=HIGHEST)]
    all_to_all x2 -> x0, starting transfers between devices: 23.9 us -> none  [the longest x1 13.3 us: per_device(): lax.all_to_all(dens_real, 'ga', split_axis=2, concat_axis=1, tiled=True)]
  transfers between devices with their start and end apart: 3 -> 0, of which waited for: 1 -> 0; matrix products, arithmetic and copies ran while one was open for 22% -> 0% of each run, Pallas kernels for 0% -> 0%
where the time goes in v1:
time: 94.7 us; the launch traced here: 94 us
  Pallas kernels  90.8 us (96%)
  local copies, waits for them, and re-layouts  1.74 us (2%)
  other arithmetic  1.46 us (2%)
    pallas_call x1, Pallas kernels, sum_up(): pl.pallas_call(sum_kernel, out_shape=(jax.ShapeDtypeStruct((BN, 16, G_DEV...  43 us
    pallas_call x1, Pallas kernels, partial_sums(): pl.pallas_call(partial_kernel, out_shape=jax.ShapeDtypeStruct((CN, YN, ZN...  25.4 us
    pallas_call x1, Pallas kernels, gather_miller(): pl.pallas_call(miller_kernel, out_shape=jax.ShapeDtypeStruct(shape, jnp.i...  20.6 us

profile of v1, /device:TPU:1, one launch (start us, length us, event | category | flops | bytes accessed | tf_op | source)
XLA Modules:
  0.0 94.0 jit_solution(10690475039966330714)
XLA Ops:
  0.0 0.9 fusion.3
  0.9 0.6 pad_add_fusion.mine_ref
  1.5 20.6 %miller_gather.1.miller_ref = s32[8,4,2,2,640]{4,3,2,1,0:T(2,128)} custom-call(s32[2,640]{1,0:T(2,128)} %pad_add_fusion.mine_ref), custom_call_target="tpu_custom_call" | custom-call | tf_op jit(solution)/shard_map/miller_gather/pallas_call | solution.py:133
  22.1 25.4 %partial_sums.1.u_ref = f32[2,4,8,16,640]{4,3,2,1,0:T(8,128)} custom-call(s32[2,8]{1,0:T(2,128)} %pair_ref.1, f32[2]{0:T(128)} %val_ref.1, f32[32]{0:T(128)} %cond_ref.1, bf16[2,2,2,18432]{3,2,1,0:T(2,128)(2,1)} %pv_ref.1, bf16[2,32,2,18432]{3,2,1,0:T(2,128)(2,1)} %pc_ref.1, bf16[2,512,512]{2,1,0:T(8,128)(2,1)} %constant.48.clone.wzh_ref, ...), custom_call_target="tpu_custom_call" | custom-call | tf_op jit(solution)/shard_map/partial_sums/pallas_call | solution.py:264
  47.4 0.0 copy-start
  47.4 1.7 %copy-done = f32[2,4,8,16,640]{4,3,2,1,0:T(8,128)S(1)} copy-done((f32[2,4,8,16,640]{4,3,2,1,0:T(8,128)S(1)}, f32[2,4,8,16,640]{4,3,2,1,0:T(8,128)}, u32[]{:S(2)}) %copy-start) | copy-done | bytes 2621464
  49.2 43.0 %sum_up.1 = (f32[4,16,640]{2,1,0:T(8,128)S(1)}, f32[2,4,2,16,128]{4,3,2,1,0:T(8,128)S(1)}) custom-call(f32[2,4,8,16,640]{4,3,2,1,0:T(8,128)S(1)} %copy-done), custom_call_target="tpu_custom_call" | custom-call | tf_op jit(solution)/shard_map/sum_up/pallas_call | solution.py:387
  92.1 1.9 %slab.1 = f32[256,2,640]{2,1,0:T(2,128)} custom-call(f32[2,4,2,16,128]{4,3,2,1,0:T(8,128)S(1)} %get-tuple-element.7.rows_ref, f32[4,16,640]{2,1,0:T(8,128)S(1)} %get-tuple-element.8.amps_ref), custom_call_target="tpu_custom_call" | custom-call | tf_op jit(solution)/shard_map/slab/pallas_call | solution.py:424
Async XLA Ops:
  47.4 1.7 %copy-start = (f32[2,4,8,16,640]{4,3,2,1,0:T(8,128)S(1)}, f32[2,4,8,16,640]{4,3,2,1,0:T(8,128)}, u32[]{:S(2)}) copy-start(f32[2,4,8,16,640]{4,3,2,1,0:T(8,128)} %partial_sums.1.u_ref) | copy-start | bytes 7864324

commit v2 on v0

v2 whole, which is shorter than its diff:
```python
import math

import jax
import jax.numpy as jnp
import numpy as np
from jax import lax
from jax.experimental import pallas as pl
from jax.experimental.pallas import tpu as pltpu
from jax.sharding import PartitionSpec as P

NX = 128
NY = 96
NZ = 192
ROW_DEV = 16
PAIRS = 8
GA = 64
ZN, YN, CN, BN = 8, 4, 2, 4
HALF_Y = NY // 2
PENCILS = NY * NZ // GA
G_DEV = 640
TILES = G_DEV // 128
MESH = pl.DeviceIdType.MESH
F32 = jnp.float32
BF16 = jnp.bfloat16


def split_np(table):
    high = table.astype(np.float32).astype(jnp.bfloat16)
    low = (table - high.astype(np.float64)).astype(jnp.bfloat16)
    return high, low


def z_table():
    points = np.arange(NZ)
    angle = 2.0 * np.pi * ((points[:, None] * points[None, :]) % NZ) / NZ
    cosine, sine = np.cos(angle), np.sin(angle)
    table = np.zeros((2, 2, 256, 2, 2, 128))
    for parity in range(2):
        rows = slice(64 * parity, 64 * parity + NZ)
        for part_in in range(2):
            for part_out in range(2):
                values = cosine if part_in == part_out else (sine if part_in else -sine)
                for half in range(2):
                    table[parity, part_in, rows, part_out, half, 0:96] = values[:, 96 * half : 96 * half + 96]
    return table.reshape(2, 512, 512)


def y_table():
    k = np.arange(NY)[:, None]
    table = np.zeros((2, NY, 2, 2, HALF_Y))
    for parity in range(2):
        y = 2 * np.arange(HALF_Y)[None, :] + parity
        angle = 2.0 * np.pi * ((k * y) % NY) / NY
        table[0, :, 0, parity] = np.cos(angle)
        table[0, :, 1, parity] = np.sin(angle)
        table[1, :, 0, parity] = -np.sin(angle)
        table[1, :, 1, parity] = np.cos(angle)
    return table.reshape(2 * NY, 4 * HALF_Y)


def x_table():
    angle = 2.0 * np.pi * np.arange(NX) / NX
    norm = 1.0 / math.sqrt(NX * NY * NZ)
    return np.tile(np.stack([np.cos(angle), np.sin(angle)]) * norm, (4, 1)).astype(np.float32)


def split(value):
    high = value.astype(BF16)
    low = (value - high.astype(F32)).astype(BF16)
    return high, low


def dot(a, b):
    return jnp.dot(a, b, preferred_element_type=F32)


def dot3(a_high, a_low, b_high, b_low):
    return dot(a_high, b_high) + (dot(a_high, b_low) + dot(a_low, b_high))


def coordinates():
    band = lax.axis_index("band")
    ga = lax.axis_index("ga")
    return band, ga // 8, (ga // 2) % 4, ga % 2


def device(band, z, y, c):
    return (band, z * 8 + y * 2 + c)


def greet(partners):
    barrier = pltpu.get_barrier_semaphore()
    for partner in partners:
        pl.semaphore_signal(barrier, inc=1, device_id=partner, device_id_type=MESH)
    pl.semaphore_wait(barrier, len(partners))


def send(src, dst, send_sem, recv_sem, partner):
    copy = pltpu.make_async_remote_copy(
        src_ref=src, dst_ref=dst, send_sem=send_sem, recv_sem=recv_sem, device_id=partner, device_id_type=MESH
    )
    copy.start()
    return copy


def density_step(first, step, chosen, pv_ref, pc_ref, dens):
    lanes = pl.ds(pl.multiple_of(step * 384, 384), 384)
    y2 = first + step
    for p in range(PAIRS):
        v, q = chosen[p]
        vr = pv_ref[0, v, :, lanes].astype(F32)
        vi = pv_ref[1, v, :, lanes].astype(F32)
        cr = pc_ref[0, q, :, lanes].astype(F32)
        ci = pc_ref[1, q, :, lanes].astype(F32)
        rows = slice(2 * p, 2 * p + 2)
        dens[y2, rows, 0:384] = vr * cr + vi * ci
        dens[y2, rows, 384:768] = vr * ci - vi * cr


def transform_planes(
    chosen, pv_refs, pc_refs, wzh_ref, wzl_ref, wyh_ref, wyl_ref, dens, zed, spec, wait_psi, wait_tables, after_density
):
    for piece in range(PIECES):
        wait_psi(piece)

        @pl.loop(0, HALF_Y // PIECES // 2)
        def _(step):
            for u in range(2):
                density_step(piece * (HALF_Y // PIECES), step * 2 + u, chosen, pv_refs[piece], pc_refs[piece], dens)

    after_density()
    wait_tables()
    for parity in range(2):
        first = 128 * parity
        both = jnp.concatenate([dens[:, :, first : first + 256], dens[:, :, 384 + first : 640 + first]], axis=2)
        high, low = split(both.reshape(768, 512))
        result = dot3(high, low, wzh_ref[parity], wzl_ref[parity])
        for tile in range(4):
            zed[parity, tile] = result[:, 128 * tile : 128 * tile + 128]
    for p in range(PAIRS):
        for plane in range(2):
            row = 2 * p + plane
            halves = [
                jnp.concatenate(
                    [
                        zed[parity, 2 * part + tile, pl.ds(row, HALF_Y, stride=16), :]
                        for part in range(2)
                        for parity in range(2)
                    ],
                    axis=0,
                )
                for tile in range(2)
            ]
            high, low = split(jnp.concatenate(halves, axis=1))
            result = dot3(wyh_ref[...], wyl_ref[...], high, low)
            for part in range(2):
                for tile in range(2):
                    spec[tile, pl.ds(part * 16 + plane * 8 + p, NY, stride=32), :] = result[
                        part * NY : (part + 1) * NY, 128 * tile : 128 * tile + 128
                    ]


def take(table, index):
    return jnp.take_along_axis(table, index, axis=1)


def partial_block(m, cd, miller_of, table, plane_of_row, scale, spec, store):
    base = pl.multiple_of(m * 96, 96)
    for g in range(TILES):
        lanes = slice(128 * g, 128 * g + 128)
        line = jnp.broadcast_to(miller_of(0, lanes), (8, 128))
        h = jnp.broadcast_to(miller_of(1, lanes), (8, 128))
        second = line >= 96
        third = line >= 192
        index = line - jnp.where(third, 192, jnp.where(second, 96, 0))
        phases = take(table, (h * plane_of_row) & 127)
        c0, s0, c1, s1 = [jnp.broadcast_to(phases[i : i + 1], (8, 128)) for i in range(4)]
        got = []
        for group in range(4):
            values = []
            for tile in range(3):
                k_row, half = (3 * cd + tile) // 2, (3 * cd + tile) % 2
                rows = pl.ds(pl.multiple_of(base + (32 * k_row + 8 * group), 8), 8)
                values.append(take(spec[half, rows, :], index))
            got.append(jnp.where(third, values[2], jnp.where(second, values[1], values[0])))
        re0, re1, im0, im1 = got
        out_re = (c0 * re0 + s0 * im0) + (c1 * re1 + s1 * im1)
        out_im = (c0 * im0 - s0 * re0) + (c1 * im1 - s1 * re1)
        store(slice(0, 8), lanes, out_re * scale)
        store(slice(8, 16), lanes, out_im * scale)


LAGS = (0, 2), (2, 0), (2, 2), (3, 2)
PIECES = 3
CHUNKS = 4
SLOTS = ZN // CHUNKS
FIRST = 3
OWN = ZN - FIRST


def main_kernel(
    pair_ref,
    val_ref,
    cond_ref,
    pv_hbm,
    pc_hbm,
    wzh_hbm,
    wzl_hbm,
    wyh_hbm,
    wyl_hbm,
    wx_ref,
    miller_ref,
    amps_ref,
    rows_ref,
    pv_refs,
    pc_refs,
    wzh_ref,
    wzl_ref,
    wyh_ref,
    wyl_ref,
    dens,
    zed,
    spec,
    lines,
    sums,
    from_core,
    relayed,
    near,
    far,
    total,
    by_z,
    amps,
    rows,
    x_out,
    x_in,
    z_out,
    z_in,
    load_sem,
    send_sem,
    recv_sem,
):
    band, z, y, c = coordinates()
    psi_loads = []
    for piece in range(PIECES):
        lanes = pl.ds(piece * (NY * NZ // PIECES), NY * NZ // PIECES)
        for n, (src, dst) in enumerate(((pv_hbm, pv_refs[piece]), (pc_hbm, pc_refs[piece]))):
            copy = pltpu.make_async_copy(src.at[:, :, :, lanes], dst, load_sem.at[2 * piece + n])
            copy.start()
            psi_loads.append(copy)
    table_loads = []
    for n, (src, dst) in enumerate(
        ((wzh_hbm, wzh_ref), (wzl_hbm, wzl_ref), (wyh_hbm, wyh_ref), (wyl_hbm, wyl_ref))
    ):
        copy = pltpu.make_async_copy(src, dst, load_sem.at[2 * PIECES + n])
        copy.start()
        table_loads.append(copy)

    def wait_psi(piece):
        for copy in psi_loads[2 * piece : 2 * piece + 2]:
            copy.wait()

    def wait_tables():
        for copy in table_loads:
            copy.wait()

    z_partners = [device(band, (z + d) % ZN, y, c) for d in range(1, ZN)]
    x_partners = [device((band + d) % BN, z, y, c) for d in range(1, BN)]
    core_partner = device(band, z, y, 1 - c)
    plane_partners = [core_partner] + [
        device(band, z, (y + d) % YN, (c + e) % CN) for d in range(1, YN) for e in range(CN)
    ]
    ahead = (y + 1 + 2 * c) % YN
    behind = (y + 3 - 2 * c) % YN
    across = (y + 2) % YN
    to_ahead = device(band, z, ahead, c)
    to_behind = device(band, z, behind, c)

    k = miller_ref[1:2, :]
    l = miller_ref[2:3, :]
    lines[z, y, c, 0:1, :] = jnp.where(k < 0, k + NY, k) * NZ + jnp.where(l < 0, l + NZ, l) - (z * 8 + y * 2 + c) * PENCILS
    lines[z, y, c, 1:2, :] = miller_ref[0:1, :] & (NX - 1)
    greet(z_partners + x_partners + plane_partners)

    sent = []

    def start(slot, src, dst, partner):
        copy = send(src, dst, send_sem.at[slot], recv_sem.at[slot], partner)
        sent.append(copy)
        return copy

    mine = lines.at[z, y, c]
    line_copies = [start(n, mine, mine, partner) for n, partner in enumerate(z_partners)]

    def pass_lines_on():
        for copy in line_copies:
            copy.wait_recv()
        block = lines.at[:, y, c]
        for n, partner in enumerate(plane_partners):
            line_copies.append(start(7 + n, block, block, partner))

    chosen = [(pair_ref[0, p] & 1, pair_ref[1, p] & 31) for p in range(PAIRS)]
    pair_rows = lax.broadcasted_iota(jnp.int32, (8, 128), 0)
    gap = jnp.ones((8, 128), F32)
    for p, (v, q) in enumerate(chosen):
        gap = jnp.where(pair_rows == p, cond_ref[q] - val_ref[v], gap)
    scale = jnp.sqrt(4.0 / (gap * math.sqrt(32.0)))
    plane_of_row = 2 * (z * 8 + y * 2 + c) + ((pair_rows >> 1) & 1)
    table = wx_ref[...]

    transform_planes(
        chosen, pv_refs, pc_refs, wzh_ref, wzl_ref, wyh_ref, wyl_ref, dens, zed, spec, wait_psi, wait_tables, pass_lines_on
    )
    for copy in line_copies[7:]:
        copy.wait_recv()

    def add_up(yd, chunk):
        @pl.loop(0, SLOTS)
        def _(step):
            slot = chunk * SLOTS + step
            zd = (z + slot + FIRST) % ZN
            for cd in range(CN):

                def miller_of(kind, lanes):
                    return lines[zd, yd, cd, kind : kind + 1, lanes]

                def store(sublanes, lanes, value):
                    sums[cd, yd, slot, sublanes, lanes] = value

                partial_block(zd * YN + yd, cd, miller_of, table, plane_of_row, scale, spec, store)

    def part(ref, chunk, *index):
        return ref.at[(*index, pl.ds(chunk * SLOTS, SLOTS))]

    def exchange(chunk, n, yd):
        slot = 14 + 7 * chunk + n
        return start(slot, part(sums, chunk, 1 - c, yd), part(from_core, chunk, yd), core_partner)

    def join(copy, chunk, yd):
        copy.wait_recv()
        part(from_core, chunk, yd)[...] += part(sums, chunk, c, yd)[...]

    flows = [{} for _ in range(CHUNKS)]

    def send_relay(chunk):
        join(flows[chunk]["core", 0], chunk, across)
        flows[chunk]["relay"] = start(
            14 + 7 * chunk + 4, part(from_core, chunk, across), part(relayed, chunk), to_ahead
        )

    def send_back(chunk):
        join(flows[chunk]["core", 1], chunk, behind)
        flows[chunk]["back"] = start(14 + 7 * chunk + 5, part(from_core, chunk, behind), part(near, chunk), to_behind)

    def send_forth(chunk):
        join(flows[chunk]["core", 2], chunk, ahead)
        flows[chunk]["relay"].wait_recv()
        part(from_core, chunk, ahead)[...] += part(relayed, chunk)[...]
        flows[chunk]["forth"] = start(14 + 7 * chunk + 6, part(from_core, chunk, ahead), part(far, chunk), to_ahead)

    along_z = 14 + 7 * CHUNKS
    z_copies = []

    def send_z(chunk):
        flows[chunk]["core", 3].wait_recv()
        part(total, chunk)[...] = part(from_core, chunk, y)[...] + part(sums, chunk, c, y)[...]
        flows[chunk]["back"].wait_recv()
        flows[chunk]["forth"].wait_recv()
        part(total, chunk)[...] += part(near, chunk)[...] + part(far, chunk)[...]
        for slot in range(chunk * SLOTS, chunk * SLOTS + SLOTS):
            if slot != OWN:
                partner = device(band, (z + slot + FIRST) % ZN, y, c)
                z_copies.append((slot, start(along_z + slot, total.at[slot], by_z.at[slot], partner)))

    order = [across, ahead, behind, y]
    plan = {}
    for chunk in range(CHUNKS):
        for (n, lag), action in zip(LAGS, (send_relay, send_back, send_forth, send_z)):
            plan.setdefault(n * CHUNKS + chunk + lag, []).append((action, chunk))
    for step in range(max(plan) + 1):
        if step < 4 * CHUNKS:
            n, chunk = divmod(step, CHUNKS)
            add_up(order[n], chunk)
            flows[chunk]["core", n] = exchange(chunk, n, order[n])
        for action, chunk in plan.get(step, []):
            action(chunk)

    x_rows = along_z + 8
    z_rows = x_rows + 3
    plane_rows = z_rows + 7
    along_x = plane_rows + 7

    def own_rows(to_band, z2):
        return total[(2 * to_band + z2 - z - FIRST + 2 * ZN) % ZN, :, 0:128]

    x_row_copies = []
    for n, partner in enumerate(x_partners):
        for z2 in range(2):
            x_out[n, z2] = own_rows((band + n + 1) % BN, z2)
        x_row_copies.append(start(x_rows + n, x_out.at[n], x_in.at[band], partner))
    for z2 in range(2):
        x_in[band, z2] = own_rows(band, z2)
    for copy in x_row_copies:
        copy.wait_recv()
    for z2 in range(2):
        parts = [x_in[b, z2] for b in range(BN)]
        for_real = [-piece for piece in parts]
        for_imag = [piece for both in parts for piece in (-both[8:16], both[0:8])]
        z_out[z2] = jnp.concatenate(for_real + for_imag, axis=0).T[0:ROW_DEV]
    z_row_copies = [start(z_rows + n, z_out, z_in.at[n], partner) for n, partner in enumerate(z_partners)]

    result = total[OWN]
    for slot, copy in z_copies:
        copy.wait_recv()
        result = result + by_z[slot]
    amps[band] = result
    amp_copies = [
        start(along_x + n, amps.at[band], amps.at[band], partner) for n, partner in enumerate(x_partners)
    ]
    own = z_out[...]
    for n, copy in enumerate(z_row_copies):
        copy.wait_recv()
        own = own + z_in[n]
    for z2 in range(2):
        rows[z2, y, c] = own[z2]
    block = rows.at[:, y, c]
    row_copies = [start(plane_rows + n, block, block, partner) for n, partner in enumerate(plane_partners)]
    for copy in amp_copies:
        copy.wait_recv()
    amps_ref[...] = amps[...]
    for copy in row_copies:
        copy.wait_recv()
    rows_ref[...] = rows[...]
    for copy in sent:
        copy.wait_send()


def amplitudes(pair_list, val_energy, cond_energy, psi_valence, psi_conduction, miller):
    vmem = pl.BlockSpec(memory_space=pltpu.VMEM)
    smem = pl.BlockSpec(memory_space=pltpu.SMEM)
    wzh, wzl = split_np(z_table())
    wyh, wyl = split_np(y_table())
    tables = [jnp.asarray(t) for t in (wzh, wzl, wyh, wyl, x_table())]
    block = (ZN, 16, G_DEV)
    return pl.pallas_call(
        main_kernel,
        out_shape=(
            jax.ShapeDtypeStruct((BN, 16, G_DEV), F32),
            jax.ShapeDtypeStruct((2, YN, CN, ROW_DEV, 128), F32),
        ),
        in_specs=[smem] * 3 + [pl.BlockSpec(memory_space=pl.ANY)] * 6 + [vmem] * 2,
        out_specs=(vmem, vmem),
        scratch_shapes=[
            [pltpu.VMEM((2, 2, 2, NY * NZ // PIECES), BF16)] * PIECES,
            [pltpu.VMEM((2, 32, 2, NY * NZ // PIECES), BF16)] * PIECES,
            pltpu.VMEM(wzh.shape, BF16),
            pltpu.VMEM(wzl.shape, BF16),
            pltpu.VMEM(wyh.shape, BF16),
            pltpu.VMEM(wyl.shape, BF16),
            pltpu.VMEM((HALF_Y, 16, 768), F32),
            pltpu.VMEM((2, 4, 768, 128), F32),
            pltpu.VMEM((2, NY * 32, 128), F32),
            pltpu.VMEM((ZN, YN, CN, 2, G_DEV), jnp.int32),
            pltpu.VMEM((CN, YN) + block, F32),
            pltpu.VMEM((YN,) + block, F32),
            pltpu.VMEM(block, F32),
            pltpu.VMEM(block, F32),
            pltpu.VMEM(block, F32),
            pltpu.VMEM(block, F32),
            pltpu.VMEM(block, F32),
            pltpu.VMEM((BN, 16, G_DEV), F32),
            pltpu.VMEM((2, YN, CN, ROW_DEV, 128), F32),
            pltpu.VMEM((BN - 1, 2, 16, 128), F32),
            pltpu.VMEM((BN, 2, 16, 128), F32),
            pltpu.VMEM((2, ROW_DEV, 128), F32),
            pltpu.VMEM((ZN - 1, 2, ROW_DEV, 128), F32),
            pltpu.SemaphoreType.DMA((2 * PIECES + 4,)),
            pltpu.SemaphoreType.DMA((14 + 7 * CHUNKS + 28,)),
            pltpu.SemaphoreType.DMA((14 + 7 * CHUNKS + 28,)),
        ],
        compiler_params=pltpu.CompilerParams(
            collective_id=0, has_side_effects=True, vmem_limit_bytes=56 * 1024 * 1024
        ),
        name="amplitudes",
    )(pair_list, val_energy, cond_energy, psi_valence, psi_conduction, *tables, miller)


def slab_kernel(rows_ref, amps_ref, out_ref):
    right_high, right_low = split(amps_ref[...].reshape(64, G_DEV))
    for part in range(2):
        left = rows_ref[...].reshape(256, 128)[:, 64 * part : 64 * part + 64]
        left_high, left_low = split(left)
        out_ref[:, part, :] = dot3(left_high, left_low, right_high, right_low)


def slab(rows, amps):
    vmem = pl.BlockSpec(memory_space=pltpu.VMEM)
    return pl.pallas_call(
        slab_kernel,
        out_shape=jax.ShapeDtypeStruct((256, 2, G_DEV), F32),
        in_specs=[vmem, vmem],
        out_specs=vmem,
        compiler_params=pltpu.CompilerParams(vmem_limit_bytes=60 * 1024 * 1024),
        name="slab",
    )(rows, amps)


def per_device(psi_valence, psi_conduction, val_energy, cond_energy, miller, pair_list):
    amps, rows = amplitudes(pair_list, val_energy, cond_energy, psi_valence, psi_conduction, miller)
    return slab(rows, amps)


def solution(mesh):
    return jax.shard_map(
        per_device,
        mesh=mesh,
        in_specs=(
            P(None, None, "ga", None),
            P(None, "band", "ga", None),
            P(),
            P("band"),
            P(None, "ga"),
            P(None, "band"),
        ),
        out_specs=P("band", None, "ga"),
        check_vma=False,
    )
```

time: 495 us -> 56.8 us (0.11); the launches traced: 486 us -> 56.7 us
  local copies, waits for them, and re-layouts: 249 us -> 0 us
  blocking collectives: 88.1 us -> 0 us
  Pallas kernels: 0 us -> 56.7 us
  waiting for transfers between devices: 56 us -> 0 us
  matrix products: 34.5 us -> 0 us
  starting transfers between devices: 24 us -> 0 us
  other arithmetic: 20.4 us -> 0 us
  between operations: 14.2 us -> 0.01 us
    unnamed x22 -> x0, local copies, waits for them, and re-layouts: 117 us -> none
    all_gather x2 -> x0, blocking collectives: 88.1 us -> none  [the longest x1 45.1 us: per_device(): lax.all_gather(rows_imag, 'ga', axis=1, tiled=True)]
    pallas_call x0 -> x2, Pallas kernels: none -> 56.7 us  [the longest x1 53.8 us: amplitudes(): pl.pallas_call(main_kernel, out_shape=(jax.ShapeDtypeStruct((BN, 16, G_DE...]
    reduce_scatter x1 -> x0, waiting for transfers between devices: 55.9 us -> none  [per_device(): lax.psum_scatter(gram_block(rows_real, rows_imag, amp_real, amp_imag), 'b...]
    reshape x4 -> x0, local copies, waits for them, and re-layouts: 53.6 us -> none  [the longest x1 18.3 us: per_device(): dens_real = dens_real.reshape(flat_shape)]
    all_to_all x5 -> x0, local copies, waits for them, and re-layouts: 47.8 us -> none  [the longest x2 25 us: per_device(): lax.all_to_all(dens_imag, 'ga', split_axis=2, concat_axis=1, tiled=True)]
    dot_general x16 -> x0, matrix products: 34.5 us -> none  [the longest x3 6.95 us: transform(): jnp.einsum(formula, imag_part, sine_table, precision=HIGHEST)]
    all_to_all x2 -> x0, starting transfers between devices: 23.9 us -> none  [the longest x1 13.3 us: per_device(): lax.all_to_all(dens_real, 'ga', split_axis=2, concat_axis=1, tiled=True)]
  transfers between devices with their start and end apart: 3 -> 0, of which waited for: 1 -> 0; matrix products, arithmetic and copies ran while one was open for 22% -> 0% of each run, Pallas kernels for 0% -> 0%
where the time goes in v2:
time: 56.8 us; the launch traced here: 56.7 us
  Pallas kernels  56.7 us (100%)
    pallas_call x1, Pallas kernels, amplitudes(): pl.pallas_call(main_kernel, out_shape=(jax.ShapeDtypeStruct((BN, 16, G_DE...  53.8 us
    pallas_call x1, Pallas kernels, slab(): pl.pallas_call(slab_kernel, out_shape=jax.ShapeDtypeStruct((256, 2, G_DEV...  2.84 us

profile of v2, /device:TPU:1, one launch (start us, length us, event | category | flops | bytes accessed | tf_op | source)
XLA Modules:
  0.0 56.7 jit_solution(7308498272872258845)
XLA Ops:
  0.0 53.8 %amplitudes.1 = (f32[4,16,640]{2,1,0:T(8,128)}, f32[2,4,2,16,128]{4,3,2,1,0:T(8,128)}) custom-call(s32[2,8]{1,0:T(2,128)} %pair_ref.1, f32[2]{0:T(128)} %val_ref.1, f32[32]{0:T(128)} %cond_ref.1, bf16[2,2,2,18432]{3,2,1,0:T(2,128)(2,1)} %pv_hbm.1, bf16[2,32,2,18432]{3,2,1,0:T(2,128)(2,1)} %pc_hbm.1, bf16[2,512,512]{2,1,0:T(8,128)(2,1)} %constant.10.clone.wzh_hbm, ...), custom_call_target="tpu_custom_call" | custom-call | tf_op jit(solution)/shard_map/amplitudes/pallas_call | solution.py:444
  53.8 2.8 %slab.1 = f32[256,2,640]{2,1,0:T(2,128)} custom-call(f32[2,4,2,16,128]{4,3,2,1,0:T(8,128)} %get-tuple-element.7.rows_ref, f32[4,16,640]{2,1,0:T(8,128)} %get-tuple-element.8.amps_ref), custom_call_target="tpu_custom_call" | custom-call | tf_op jit(solution)/shard_map/slab/pallas_call | solution.py:497

commit v3 on v2

--- a/solution.py
+++ b/solution.py
@@ -164,25 +164,43 @@
     return jnp.take_along_axis(table, index, axis=1)
 
 
-def partial_block(m, cd, miller_of, table, plane_of_row, scale, spec, store):
+PICK = 384
+
+
+def partial_block(m, cd, tiles, miller_of, table, plane_of_row, scale, spec, store):
     base = pl.multiple_of(m * 96, 96)
-    for g in range(TILES):
+    line = miller_of(0, slice(0, G_DEV))
+    second = line >= 96
+    third = line >= 192
+    sources = []
+    for tile in range(3):
+        k_row, half = (3 * cd + tile) // 2, (3 * cd + tile) % 2
+        sources.append(spec[half, pl.ds(pl.multiple_of(base + 32 * k_row, 32), 32), :])
+    if tiles[-1] * 128 >= PICK:
+        key = line[:, PICK:] + jnp.where(third[:, PICK:], 64, jnp.where(second[:, PICK:], 32, 0))
+        wide = G_DEV - PICK
+        ones = jnp.where(
+            lax.broadcasted_iota(jnp.int32, (384, wide), 0) == jnp.broadcast_to(key, (384, wide)), 1.0, 0.0
+        ).astype(BF16)
+        high, low = split(jnp.concatenate(sources, axis=1))
+        picked = dot(jnp.concatenate([high, low], axis=0), ones)
+        picked = picked[0:32] + picked[32:64]
+    for g in tiles:
         lanes = slice(128 * g, 128 * g + 128)
-        line = jnp.broadcast_to(miller_of(0, lanes), (8, 128))
         h = jnp.broadcast_to(miller_of(1, lanes), (8, 128))
-        second = line >= 96
-        third = line >= 192
-        index = line - jnp.where(third, 192, jnp.where(second, 96, 0))
         phases = take(table, (h * plane_of_row) & 127)
         c0, s0, c1, s1 = [jnp.broadcast_to(phases[i : i + 1], (8, 128)) for i in range(4)]
         got = []
-        for group in range(4):
-            values = []
-            for tile in range(3):
-                k_row, half = (3 * cd + tile) // 2, (3 * cd + tile) % 2
-                rows = pl.ds(pl.multiple_of(base + (32 * k_row + 8 * group), 8), 8)
-                values.append(take(spec[half, rows, :], index))
-            got.append(jnp.where(third, values[2], jnp.where(second, values[1], values[0])))
+        if 128 * g < PICK:
+            in_second = jnp.broadcast_to(line[:, lanes], (8, 128)) >= 96
+            in_third = jnp.broadcast_to(line[:, lanes], (8, 128)) >= 192
+            index = jnp.broadcast_to(line[:, lanes], (8, 128)) - jnp.where(in_third, 192, jnp.where(in_second, 96, 0))
+            for group in range(4):
+                values = [take(source[8 * group : 8 * group + 8], index) for source in sources]
+                got.append(jnp.where(in_third, values[2], jnp.where(in_second, values[1], values[0])))
+        else:
+            columns = slice(128 * g - PICK, 128 * g - PICK + 128)
+            got = [picked[8 * group : 8 * group + 8, columns] for group in range(4)]
         re0, re1, im0, im1 = got
         out_re = (c0 * re0 + s0 * im0) + (c1 * re1 + s1 * im1)
         out_im = (c0 * im0 - s0 * re0) + (c1 * im1 - s1 * re1)
@@ -190,6 +208,7 @@
         store(slice(8, 16), lanes, out_im * scale)
 
 
+ROWS_AT = (2, 5, 9)
 LAGS = (0, 2), (2, 0), (2, 2), (3, 2)
 PIECES = 3
 CHUNKS = 4
@@ -313,10 +332,82 @@
     for copy in line_copies[7:]:
         copy.wait_recv()
 
-    def add_up(yd, chunk):
-        @pl.loop(0, SLOTS)
-        def _(step):
-            slot = chunk * SLOTS + step
+    def place(n):
+        return jnp.where(n == 0, across, jnp.where(n == 1, ahead, jnp.where(n == 2, behind, y)))
+
+    def part(ref, chunk, *index):
+        return ref.at[(*index, pl.ds(chunk * SLOTS, SLOTS), slice(None), pl.ds(128, G_DEV - 128))]
+
+    def early(ref, *index):
+        return ref.at[(*index, slice(None), slice(None), pl.ds(0, 128))]
+
+    def remote(slot, src, dst, partner):
+        return pltpu.make_async_remote_copy(
+            src_ref=src,
+            dst_ref=dst,
+            send_sem=send_sem.at[slot],
+            recv_sem=recv_sem.at[slot],
+            device_id=partner,
+            device_id_type=MESH,
+        )
+
+    def core_copy(n, chunk):
+        yd = place(n)
+        return remote(14 + 7 * chunk + n, part(sums, chunk, 1 - c, yd), part(from_core, chunk, yd), core_partner)
+
+    def relay_copy(chunk):
+        return remote(14 + 7 * chunk + 4, part(from_core, chunk, across), part(relayed, chunk), to_ahead)
+
+    def back_copy(chunk):
+        return remote(14 + 7 * chunk + 5, part(from_core, chunk, behind), part(near, chunk), to_behind)
+
+    def forth_copy(chunk):
+        return remote(14 + 7 * chunk + 6, part(from_core, chunk, ahead), part(far, chunk), to_ahead)
+
+    along_z = 14 + 7 * CHUNKS
+
+    def z_copy(slot):
+        return remote(
+            along_z + slot, total.at[slot], by_z.at[slot], device(band, (z + slot + FIRST) % ZN, y, c)
+        )
+
+    def join(n, chunk, yd):
+        core_copy(n, chunk).wait_recv()
+        part(from_core, chunk, yd)[...] += part(sums, chunk, c, yd)[...]
+
+    def send_relay(chunk):
+        join(0, chunk, across)
+        relay_copy(chunk).start()
+
+    def send_back(chunk):
+        join(1, chunk, behind)
+        back_copy(chunk).start()
+
+    def send_forth(chunk):
+        join(2, chunk, ahead)
+        relay_copy(chunk).wait_recv()
+        part(from_core, chunk, ahead)[...] += part(relayed, chunk)[...]
+        forth_copy(chunk).start()
+
+    def send_z(chunk):
+        core_copy(3, chunk).wait_recv()
+        part(total, chunk)[...] = part(from_core, chunk, y)[...] + part(sums, chunk, c, y)[...]
+        back_copy(chunk).wait_recv()
+        forth_copy(chunk).wait_recv()
+        part(total, chunk)[...] += part(near, chunk)[...] + part(far, chunk)[...]
+        for i in range(SLOTS):
+            slot = chunk * SLOTS + i
+
+            @pl.when(slot != OWN)
+            def _():
+                z_copy(slot).start()
+
+    steps = 4 * CHUNKS
+    actions = [(n * CHUNKS + lag, action) for (n, lag), action in zip(LAGS, (send_relay, send_back, send_forth, send_z))]
+
+    def add_up(n, slots, tiles):
+        yd = place(n)
+        for slot in slots:
             zd = (z + slot + FIRST) % ZN
             for cd in range(CN):
 
@@ -326,96 +417,93 @@
                 def store(sublanes, lanes, value):
                     sums[cd, yd, slot, sublanes, lanes] = value
 
-                partial_block(zd * YN + yd, cd, miller_of, table, plane_of_row, scale, spec, store)
-
-    def part(ref, chunk, *index):
-        return ref.at[(*index, pl.ds(chunk * SLOTS, SLOTS))]
-
-    def exchange(chunk, n, yd):
-        slot = 14 + 7 * chunk + n
-        return start(slot, part(sums, chunk, 1 - c, yd), part(from_core, chunk, yd), core_partner)
-
-    def join(copy, chunk, yd):
-        copy.wait_recv()
-        part(from_core, chunk, yd)[...] += part(sums, chunk, c, yd)[...]
-
-    flows = [{} for _ in range(CHUNKS)]
-
-    def send_relay(chunk):
-        join(flows[chunk]["core", 0], chunk, across)
-        flows[chunk]["relay"] = start(
-            14 + 7 * chunk + 4, part(from_core, chunk, across), part(relayed, chunk), to_ahead
-        )
-
-    def send_back(chunk):
-        join(flows[chunk]["core", 1], chunk, behind)
-        flows[chunk]["back"] = start(14 + 7 * chunk + 5, part(from_core, chunk, behind), part(near, chunk), to_behind)
-
-    def send_forth(chunk):
-        join(flows[chunk]["core", 2], chunk, ahead)
-        flows[chunk]["relay"].wait_recv()
-        part(from_core, chunk, ahead)[...] += part(relayed, chunk)[...]
-        flows[chunk]["forth"] = start(14 + 7 * chunk + 6, part(from_core, chunk, ahead), part(far, chunk), to_ahead)
-
-    along_z = 14 + 7 * CHUNKS
-    z_copies = []
-
-    def send_z(chunk):
-        flows[chunk]["core", 3].wait_recv()
-        part(total, chunk)[...] = part(from_core, chunk, y)[...] + part(sums, chunk, c, y)[...]
-        flows[chunk]["back"].wait_recv()
-        flows[chunk]["forth"].wait_recv()
-        part(total, chunk)[...] += part(near, chunk)[...] + part(far, chunk)[...]
-        for slot in range(chunk * SLOTS, chunk * SLOTS + SLOTS):
-            if slot != OWN:
-                partner = device(band, (z + slot + FIRST) % ZN, y, c)
-                z_copies.append((slot, start(along_z + slot, total.at[slot], by_z.at[slot], partner)))
-
-    order = [across, ahead, behind, y]
-    plan = {}
-    for chunk in range(CHUNKS):
-        for (n, lag), action in zip(LAGS, (send_relay, send_back, send_forth, send_z)):
-            plan.setdefault(n * CHUNKS + chunk + lag, []).append((action, chunk))
-    for step in range(max(plan) + 1):
-        if step < 4 * CHUNKS:
-            n, chunk = divmod(step, CHUNKS)
-            add_up(order[n], chunk)
-            flows[chunk]["core", n] = exchange(chunk, n, order[n])
-        for action, chunk in plan.get(step, []):
-            action(chunk)
+                partial_block(zd * YN + yd, cd, tiles, miller_of, table, plane_of_row, scale, spec, store)
 
     x_rows = along_z + 8
     z_rows = x_rows + 3
     plane_rows = z_rows + 7
     along_x = plane_rows + 7
+    early_at = along_x + 3
+
+    def early_core(n):
+        yd = place(n)
+        return remote(early_at + n, early(sums, 1 - c, yd), early(from_core, yd), core_partner)
+
+    def early_join(n, yd):
+        early_core(n).wait_recv()
+        early(from_core, yd)[...] += early(sums, c, yd)[...]
+
+    early_relay = remote(early_at + 4, early(from_core, across), early(relayed), to_ahead)
+    early_back = remote(early_at + 5, early(from_core, behind), early(near), to_behind)
+    early_forth = remote(early_at + 6, early(from_core, ahead), early(far), to_ahead)
+
+    @pl.loop(0, 4)
+    def _(n):
+        @pl.loop(0, 2)
+        def _(half):
+            add_up(n, [half * 4 + i for i in range(4)], [0])
+
+        early_core(n).start()
+
+    early_join(0, across)
+    early_relay.start()
+    early_join(1, behind)
+    early_back.start()
 
     def own_rows(to_band, z2):
         return total[(2 * to_band + z2 - z - FIRST + 2 * ZN) % ZN, :, 0:128]
 
-    x_row_copies = []
-    for n, partner in enumerate(x_partners):
+    x_row_copies = [remote(x_rows + n, x_out.at[n], x_in.at[band], partner) for n, partner in enumerate(x_partners)]
+    z_row_copies = [remote(z_rows + n, z_out, z_in.at[n], partner) for n, partner in enumerate(z_partners)]
+
+    def rows_y():
+        early_join(2, ahead)
+        early_relay.wait_recv()
+        early(from_core, ahead)[...] += early(relayed)[...]
+        early_forth.start()
+
+    def rows_x():
+        early_core(3).wait_recv()
+        early_back.wait_recv()
+        early_forth.wait_recv()
+        early(total)[...] = (early(from_core, y)[...] + early(sums, c, y)[...]) + (early(near)[...] + early(far)[...])
+        for n in range(BN - 1):
+            for z2 in range(2):
+                x_out[n, z2] = own_rows((band + n + 1) % BN, z2)
+            x_row_copies[n].start()
         for z2 in range(2):
-            x_out[n, z2] = own_rows((band + n + 1) % BN, z2)
-        x_row_copies.append(start(x_rows + n, x_out.at[n], x_in.at[band], partner))
-    for z2 in range(2):
-        x_in[band, z2] = own_rows(band, z2)
-    for copy in x_row_copies:
-        copy.wait_recv()
-    for z2 in range(2):
-        parts = [x_in[b, z2] for b in range(BN)]
-        for_real = [-piece for piece in parts]
-        for_imag = [piece for both in parts for piece in (-both[8:16], both[0:8])]
-        z_out[z2] = jnp.concatenate(for_real + for_imag, axis=0).T[0:ROW_DEV]
-    z_row_copies = [start(z_rows + n, z_out, z_in.at[n], partner) for n, partner in enumerate(z_partners)]
-
-    result = total[OWN]
-    for slot, copy in z_copies:
-        copy.wait_recv()
-        result = result + by_z[slot]
-    amps[band] = result
-    amp_copies = [
-        start(along_x + n, amps.at[band], amps.at[band], partner) for n, partner in enumerate(x_partners)
-    ]
+            x_in[band, z2] = own_rows(band, z2)
+
+    def rows_z():
+        for copy in x_row_copies:
+            copy.wait_recv()
+        for z2 in range(2):
+            parts = [x_in[b, z2] for b in range(BN)]
+            for_real = [-piece for piece in parts]
+            for_imag = [piece for both in parts for piece in (-both[8:16], both[0:8])]
+            z_out[z2] = jnp.concatenate(for_real + for_imag, axis=0).T[0:ROW_DEV]
+        for copy in z_row_copies:
+            copy.start()
+
+    @pl.loop(0, steps)
+    def _(step):
+        n = step // CHUNKS
+        chunk = step % CHUNKS
+        add_up(n, [chunk * SLOTS + i for i in range(SLOTS)], [1, 2, 3, 4])
+        core_copy(n, chunk).start()
+        for at, action in zip(ROWS_AT, (rows_y, rows_x, rows_z)):
+            pl.when(step == at)(action)
+        for first, action in actions:
+
+            @pl.when((step >= first) & (step < first + CHUNKS))
+            def _():
+                action(step - first)
+
+    for step in range(steps, steps + 2 * CHUNKS):
+        for first, action in actions:
+            if first <= step < first + CHUNKS:
+                action(step - first)
+
     own = z_out[...]
     for n, copy in enumerate(z_row_copies):
         copy.wait_recv()
@@ -424,6 +512,15 @@
         rows[z2, y, c] = own[z2]
     block = rows.at[:, y, c]
     row_copies = [start(plane_rows + n, block, block, partner) for n, partner in enumerate(plane_partners)]
+    result = total[OWN]
+    for slot in range(ZN):
+        if slot != OWN:
+            z_copy(slot).wait_recv()
+            result = result + by_z[slot]
+    amps[band] = result
+    amp_copies = [
+        start(along_x + n, amps.at[band], amps.at[band], partner) for n, partner in enumerate(x_partners)
+    ]
     for copy in amp_copies:
         copy.wait_recv()
     amps_ref[...] = amps[...]
@@ -431,6 +528,14 @@
         copy.wait_recv()
     rows_ref[...] = rows[...]
     for copy in sent:
+        copy.wait_send()
+    for chunk in range(CHUNKS):
+        for copy in [core_copy(n, chunk) for n in range(4)] + [relay_copy(chunk), back_copy(chunk), forth_copy(chunk)]:
+            copy.wait_send()
+    for slot in range(ZN):
+        if slot != OWN:
+            z_copy(slot).wait_send()
+    for copy in [early_core(n) for n in range(4)] + [early_relay, early_back, early_forth] + x_row_copies + z_row_copies:
         copy.wait_send()
 
 
@@ -474,8 +579,8 @@
             pltpu.VMEM((2, ROW_DEV, 128), F32),
             pltpu.VMEM((ZN - 1, 2, ROW_DEV, 128), F32),
             pltpu.SemaphoreType.DMA((2 * PIECES + 4,)),
-            pltpu.SemaphoreType.DMA((14 + 7 * CHUNKS + 28,)),
-            pltpu.SemaphoreType.DMA((14 + 7 * CHUNKS + 28,)),
+            pltpu.SemaphoreType.DMA((14 + 7 * CHUNKS + 35,)),
+            pltpu.SemaphoreType.DMA((14 + 7 * CHUNKS + 35,)),
         ],
         compiler_params=pltpu.CompilerParams(
             collective_id=0, has_side_effects=True, vmem_limit_bytes=56 * 1024 * 1024

time: 56.8 us -> 55.6 us (0.979)
  Pallas kernels: 56.7 us -> 55.3 us
    pallas_call x1, Pallas kernels: 53.8 us -> 52.4 us  [amplitudes(): pl.pallas_call(main_kernel, out_shape=(jax.ShapeDtypeStruct((BN, 16, G_DE...]
where the time goes in v3:
time: 55.6 us; the launch traced here: 55.3 us
  Pallas kernels  55.3 us (99%)
    pallas_call x1, Pallas kernels, amplitudes(): pl.pallas_call(main_kernel, out_shape=(jax.ShapeDtypeStruct((BN, 16, G_DE...  52.4 us
    pallas_call x1, Pallas kernels, slab(): pl.pallas_call(slab_kernel, out_shape=jax.ShapeDtypeStruct((256, 2, G_DEV...  2.84 us

profile of v3, /device:TPU:1, one launch (start us, length us, event | category | flops | bytes accessed | tf_op | source)
XLA Modules:
  0.0 55.3 jit_solution(17155054224799948685)
XLA Ops:
  0.0 52.4 %amplitudes.1 = (f32[4,16,640]{2,1,0:T(8,128)}, f32[2,4,2,16,128]{4,3,2,1,0:T(8,128)}) custom-call(s32[2,8]{1,0:T(2,128)} %pair_ref.1, f32[2]{0:T(128)} %val_ref.1, f32[32]{0:T(128)} %cond_ref.1, bf16[2,2,2,18432]{3,2,1,0:T(2,128)(2,1)} %pv_hbm.1, bf16[2,32,2,18432]{3,2,1,0:T(2,128)(2,1)} %pc_hbm.1, bf16[2,512,512]{2,1,0:T(8,128)(2,1)} %constant.10.clone.wzh_hbm, ...), custom_call_target="tpu_custom_call" | custom-call | tf_op jit(solution)/shard_map/amplitudes/pallas_call | solution.py:549
  52.4 2.8 %slab.1 = f32[256,2,640]{2,1,0:T(2,128)} custom-call(f32[2,4,2,16,128]{4,3,2,1,0:T(8,128)} %get-tuple-element.7.rows_ref, f32[4,16,640]{2,1,0:T(8,128)} %get-tuple-element.8.amps_ref), custom_call_target="tpu_custom_call" | custom-call | tf_op jit(solution)/shard_map/slab/pallas_call | solution.py:602

commit v4 on v3

--- a/solution.py
+++ b/solution.py
@@ -92,7 +92,7 @@
     barrier = pltpu.get_barrier_semaphore()
     for partner in partners:
         pl.semaphore_signal(barrier, inc=1, device_id=partner, device_id_type=MESH)
-    pl.semaphore_wait(barrier, len(partners))
+    return lambda: pl.semaphore_wait(barrier, len(partners))
 
 
 def send(src, dst, send_sem, recv_sem, partner):
@@ -259,6 +259,13 @@
     recv_sem,
 ):
     band, z, y, c = coordinates()
+    z_partners = [device(band, (z + d) % ZN, y, c) for d in range(1, ZN)]
+    x_partners = [device((band + d) % BN, z, y, c) for d in range(1, BN)]
+    core_partner = device(band, z, y, 1 - c)
+    plane_partners = [core_partner] + [
+        device(band, z, (y + d) % YN, (c + e) % CN) for d in range(1, YN) for e in range(CN)
+    ]
+    wait_for_partners = greet(z_partners + x_partners + plane_partners)
     psi_loads = []
     for piece in range(PIECES):
         lanes = pl.ds(piece * (NY * NZ // PIECES), NY * NZ // PIECES)
@@ -282,12 +289,6 @@
         for copy in table_loads:
             copy.wait()
 
-    z_partners = [device(band, (z + d) % ZN, y, c) for d in range(1, ZN)]
-    x_partners = [device((band + d) % BN, z, y, c) for d in range(1, BN)]
-    core_partner = device(band, z, y, 1 - c)
-    plane_partners = [core_partner] + [
-        device(band, z, (y + d) % YN, (c + e) % CN) for d in range(1, YN) for e in range(CN)
-    ]
     ahead = (y + 1 + 2 * c) % YN
     behind = (y + 3 - 2 * c) % YN
     across = (y + 2) % YN
@@ -298,7 +299,7 @@
     l = miller_ref[2:3, :]
     lines[z, y, c, 0:1, :] = jnp.where(k < 0, k + NY, k) * NZ + jnp.where(l < 0, l + NZ, l) - (z * 8 + y * 2 + c) * PENCILS
     lines[z, y, c, 1:2, :] = miller_ref[0:1, :] & (NX - 1)
-    greet(z_partners + x_partners + plane_partners)
+    wait_for_partners()
 
     sent = []
 
@@ -591,10 +592,10 @@
 
 def slab_kernel(rows_ref, amps_ref, out_ref):
     right_high, right_low = split(amps_ref[...].reshape(64, G_DEV))
+    right = jnp.concatenate([right_high, right_low, right_high], axis=0)
     for part in range(2):
-        left = rows_ref[...].reshape(256, 128)[:, 64 * part : 64 * part + 64]
-        left_high, left_low = split(left)
-        out_ref[:, part, :] = dot3(left_high, left_low, right_high, right_low)
+        left_high, left_low = split(rows_ref[...].reshape(256, 128)[:, 64 * part : 64 * part + 64])
+        out_ref[:, part, :] = dot(jnp.concatenate([left_high, left_high, left_low], axis=1), right)
 
 
 def slab(rows, amps):

time: 55.6 us -> 55.3 us (level)
  no operation moved by 1% of the time
where the time goes in v4:
time: 55.3 us; the launch traced here: 55.1 us
  Pallas kernels  55 us (99%)
    pallas_call x1, Pallas kernels, amplitudes(): pl.pallas_call(main_kernel, out_shape=(jax.ShapeDtypeStruct((BN, 16, G_DE...  52.5 us
    pallas_call x1, Pallas kernels, slab(): pl.pallas_call(slab_kernel, out_shape=jax.ShapeDtypeStruct((256, 2, G_DEV...  2.56 us

profile of v4, /device:TPU:1, one launch (start us, length us, event | category | flops | bytes accessed | tf_op | source)
XLA Modules:
  0.0 55.1 jit_solution(17666929627946035957)
XLA Ops:
  0.0 52.5 %amplitudes.1 = (f32[4,16,640]{2,1,0:T(8,128)}, f32[2,4,2,16,128]{4,3,2,1,0:T(8,128)}) custom-call(s32[2,8]{1,0:T(2,128)} %pair_ref.1, f32[2]{0:T(128)} %val_ref.1, f32[32]{0:T(128)} %cond_ref.1, bf16[2,2,2,18432]{3,2,1,0:T(2,128)(2,1)} %pv_hbm.1, bf16[2,32,2,18432]{3,2,1,0:T(2,128)(2,1)} %pc_hbm.1, bf16[2,512,512]{2,1,0:T(8,128)(2,1)} %constant.10.clone.wzh_hbm, ...), custom_call_target="tpu_custom_call" | custom-call | tf_op jit(solution)/shard_map/amplitudes/pallas_call | solution.py:550
  52.5 2.6 %slab.1 = f32[256,2,640]{2,1,0:T(2,128)} custom-call(f32[2,4,2,16,128]{4,3,2,1,0:T(8,128)} %get-tuple-element.7.rows_ref, f32[4,16,640]{2,1,0:T(8,128)} %get-tuple-element.8.amps_ref), custom_call_target="tpu_custom_call" | custom-call | tf_op jit(solution)/shard_map/slab/pallas_call | solution.py:603

commit v5 on v4

--- a/solution.py
+++ b/solution.py
@@ -210,7 +210,7 @@
 
 ROWS_AT = (2, 5, 9)
 LAGS = (0, 2), (2, 0), (2, 2), (3, 2)
-PIECES = 3
+PIECES = 6
 CHUNKS = 4
 SLOTS = ZN // CHUNKS
 FIRST = 3

time: 55.3 us -> 55.4 us (level)
  no operation moved by 1% of the time
where the time goes in v5:
time: 55.4 us; the launch traced here: 55.1 us
  Pallas kernels  55.1 us (99%)
    pallas_call x1, Pallas kernels, amplitudes(): pl.pallas_call(main_kernel, out_shape=(jax.ShapeDtypeStruct((BN, 16, G_DE...  52.5 us
    pallas_call x1, Pallas kernels, slab(): pl.pallas_call(slab_kernel, out_shape=jax.ShapeDtypeStruct((256, 2, G_DEV...  2.56 us

profile of v5, /device:TPU:1, one launch (start us, length us, event | category | flops | bytes accessed | tf_op | source)
XLA Modules:
  0.0 55.1 jit_solution(4250288565962801514)
XLA Ops:
  0.0 52.5 %amplitudes.1 = (f32[4,16,640]{2,1,0:T(8,128)}, f32[2,4,2,16,128]{4,3,2,1,0:T(8,128)}) custom-call(s32[2,8]{1,0:T(2,128)} %pair_ref.1, f32[2]{0:T(128)} %val_ref.1, f32[32]{0:T(128)} %cond_ref.1, bf16[2,2,2,18432]{3,2,1,0:T(2,128)(2,1)} %pv_hbm.1, bf16[2,32,2,18432]{3,2,1,0:T(2,128)(2,1)} %pc_hbm.1, bf16[2,512,512]{2,1,0:T(8,128)(2,1)} %constant.10.clone.wzh_hbm, ...), custom_call_target="tpu_custom_call" | custom-call | tf_op jit(solution)/shard_map/amplitudes/pallas_call | solution.py:550
  52.5 2.6 %slab.1 = f32[256,2,640]{2,1,0:T(2,128)} custom-call(f32[2,4,2,16,128]{4,3,2,1,0:T(8,128)} %get-tuple-element.7.rows_ref, f32[4,16,640]{2,1,0:T(8,128)} %get-tuple-element.8.amps_ref), custom_call_target="tpu_custom_call" | custom-call | tf_op jit(solution)/shard_map/slab/pallas_call | solution.py:603
